TPU v7x, 32 devices: a whole 2x2x4 slice. The times are simulated.
32 devices in a mesh: row: 8 (over z, x), col: 4 (over y, core).
Axes of the slice: x: 2, y: 2, z: 4, core: 2. Of those that a mesh axis runs over, the one named last changes fastest.
Arguments:
- eigvecs: float32 [2048, 65536], P(('col', 'row')), may hold values from -6 to 6
- reflectors: float32 [4, 256, 65536], P(None, 'col', 'row'), may hold values from -0.0234375 to 0.0234375
- tfactors: float32 [4, 256, 256], replicated, may hold values from -0.5 to 2, as said below
Outputs:
- backed: float32 [65536, 2048], P('row', 'col')
Inputs may be any that keep to these rules, and one draw needn't show every extreme that they name: `tfactors`: each block's factor is upper triangular with diagonal entries between 1 and 2.
All inputs are finite; a program needn't handle non-finite values.
Results may differ from a plain program's by a relative error of at most 0.0001.
Values sent between devices are 32-bit elements; how exact they have to be, the bound alone decides.
A program may use at most 128 MiB of HBM per device.

v0:
```python
import jax
import jax.numpy as jnp
from jax import lax
from jax.sharding import PartitionSpec as P


def matmul(left, right):
    return jnp.dot(left, right, precision=lax.Precision.HIGHEST, preferred_element_type=jnp.float32)


def inner_rows(left, right):
    return lax.dot_general(
        left,
        right,
        (((0,), (0,)), ((), ())),
        precision=lax.Precision.HIGHEST,
        preferred_element_type=jnp.float32,
    )


def body(eigvecs, reflectors, tfactors):
    arrived = lax.all_to_all(eigvecs, "row", split_axis=1, concat_axis=0, tiled=True)
    current = arrived.T
    blocks = tfactors.shape[0]
    for block in range(blocks - 1, -1, -1):
        vectors = lax.all_gather(reflectors[block], "col", axis=0, tiled=True)
        inner_part = matmul(vectors, current)
        inner_sum = lax.psum(inner_part, "row")
        scaled = matmul(tfactors[block], inner_sum)
        current = current - inner_rows(vectors, scaled)
    return current


def solution(mesh):
    in_specs = (P(("col", "row"), None), P(None, "col", "row"), P())
    out_specs = P("row", "col")
    return jax.shard_map(body, mesh=mesh, in_specs=in_specs, out_specs=out_specs, check_vma=False)
```

profile of v0, /device:TPU:0, one launch (start us, length us, event | category | flops | bytes accessed | tf_op | source)
XLA Modules:
  0.0 982.1 jit_solution(12616680192022693570)
XLA Ops:
  6.5 11.7 %copy.8 = f32[8,8,8,8192]{3,2,0,1:T(8,128)} copy(f32[8,8,8,8192]{3,2,1,0:T(8,128)} %bitcast.66) | data formatting | bytes 33554432 | tf_op jit(solution)/shard_map/all_to_all | solution.py:22
  18.2 7.3 all-to-all-start
  25.5 6.9 fusion.33
  32.4 0.0 all-reduce.5.cloned.1.call-start
  32.5 59.8 %all-gather.9.cloned.1.call-done = f32[1,256,8192]{2,1,0:T(8,128)} async-done(((f32[1,64,8192]{2,1,0:T(8,128)}), f32[1,256,8192]{2,1,0:T(8,128)}) %all-gather.9.cloned.1.call-update) | async-done | bytes 8388624 | tf_op jit(solution)/shard_map/all_gather | solution.py:26
  92.3 296.3 %all-to-all-done = f32[64,8,8192]{2,0,1:T(8,128)} async-done(((f32[64,8,8192]{2,0,1:T(8,128)}), f32[64,8,8192]{2,0,1:T(8,128)}, u32[]{:S(2)}, u32[]{:S(2)}) %all-to-all-start) | async-done | bytes 16777248 | tf_op jit(solution)/shard_map/all_to_all | solution.py:22
  388.5 19.4 %fusion.10 = f32[256,512]{1,0:T(8,128)} fusion(f32[512,8192]{1,0:T(8,128)} %bitcast.1, f32[1,256,8192]{2,1,0:T(8,128)} %all-gather.9.cloned.1.call-done), kind=kOutput, calls=%fused_computation.15 | convolution fusion | flops 12884901888 | bytes 25690112 | tf_op jit(solution)/shard_map/dot_general | solution.py:8
  408.1 0.7 all-gather.11.cloned.1.call-update
  408.7 0.2 all-reduce.7.cloned.1.call-start
  409.0 70.6 %all-reduce.5.cloned.1.call-done = f32[256,512]{1,0:T(8,128)} async-done(((f32[256,512]{1,0:T(8,128)}), f32[256,512]{1,0:T(8,128)}) %all-reduce.5.cloned.1.call-update) | async-done | bytes 524304 | tf_op jit(solution)/shard_map/psum | solution.py:28
  479.6 2.0 fusion.27
  481.6 25.9 %convolution_subtract_fusion.2 = f32[512,8192]{1,0:T(8,128)} fusion(f32[512,8192]{1,0:T(8,128)} %bitcast.1, f32[512,256]{1,0:T(8,128)S(1)} %fusion.27, f32[1,256,8192]{2,1,0:T(8,128)} %all-gather.9.cloned.1.call-done), kind=kOutput, calls=%fused_computation.4 | convolution fusion | flops 12889096192 | bytes 42467328 | tf_op jit(solution)/shard_map/dot_general | solution.py:12
  507.5 31.3 %all-gather.11.cloned.1.call-done = f32[1,256,8192]{2,1,0:T(8,128)} async-done(((f32[1,64,8192]{2,1,0:T(8,128)}), f32[1,256,8192]{2,1,0:T(8,128)}) %all-gather.11.cloned.1.call-update) | async-done | bytes 8388624 | tf_op jit(solution)/shard_map/all_gather | solution.py:26
  538.8 18.4 %fusion.12 = f32[256,512]{0,1:T(8,128)} fusion(f32[512,8192]{1,0:T(8,128)} %convolution_subtract_fusion.2, f32[1,256,8192]{2,1,0:T(8,128)} %all-gather.11.cloned.1.call-done), kind=kOutput, calls=%fused_computation.17 | convolution fusion | flops 12884901888 | bytes 25690112 | tf_op jit(solution)/shard_map/dot_general | solution.py:8
  557.3 0.5 all-gather.13.cloned.1.call-update
  557.9 0.3 all-reduce.9.cloned.1.call-start
  558.1 71.6 %all-reduce.7.cloned.1.call-done = f32[256,512]{0,1:T(8,128)} async-done(((f32[256,512]{0,1:T(8,128)}), f32[256,512]{0,1:T(8,128)}) %all-reduce.7.cloned.1.call-update) | async-done | bytes 524304 | tf_op jit(solution)/shard_map/psum | solution.py:28
  629.7 1.7 fusion.25
  631.4 25.9 %convolution_subtract_fusion.1 = f32[512,8192]{1,0:T(8,128)} fusion(f32[512,8192]{1,0:T(8,128)} %convolution_subtract_fusion.2, f32[512,256]{1,0:T(8,128)S(1)} %fusion.25, f32[1,256,8192]{2,1,0:T(8,128)} %all-gather.11.cloned.1.call-done), kind=kOutput, calls=%fused_computation.3 | convolution fusion | flops 12889096192 | bytes 42467328 | tf_op jit(solution)/shard_map/dot_general | solution.py:12
  657.3 31.4 %all-gather.13.cloned.1.call-done = f32[1,256,8192]{2,1,0:T(8,128)} async-done(((f32[1,64,8192]{2,1,0:T(8,128)}), f32[1,256,8192]{2,1,0:T(8,128)}) %all-gather.13.cloned.1.call-update) | async-done | bytes 8388624 | tf_op jit(solution)/shard_map/all_gather | solution.py:26
  688.7 18.4 %fusion.15 = f32[256,512]{0,1:T(8,128)} fusion(f32[512,8192]{1,0:T(8,128)} %convolution_subtract_fusion.1, f32[1,256,8192]{2,1,0:T(8,128)} %all-gather.13.cloned.1.call-done), kind=kOutput, calls=%fused_computation.18 | convolution fusion | flops 12884901888 | bytes 25690112 | tf_op jit(solution)/shard_map/dot_general | solution.py:8
  707.2 0.7 all-gather.15.cloned.1.call-update
  707.9 0.4 all-reduce.11.cloned.1.call-start
  708.4 71.3 %all-reduce.9.cloned.1.call-done = f32[256,512]{0,1:T(8,128)} async-done(((f32[256,512]{0,1:T(8,128)}), f32[256,512]{0,1:T(8,128)}) %all-reduce.9.cloned.1.call-update) | async-done | bytes 524304 | tf_op jit(solution)/shard_map/psum | solution.py:28
  779.7 1.7 fusion.23
  781.4 25.9 %convolution_subtract_fusion = f32[512,8192]{1,0:T(8,128)} fusion(f32[512,8192]{1,0:T(8,128)} %convolution_subtract_fusion.1, f32[512,256]{1,0:T(8,128)S(1)} %fusion.23, f32[1,256,8192]{2,1,0:T(8,128)} %all-gather.13.cloned.1.call-done), kind=kOutput, calls=%fused_computation.2 | convolution fusion | flops 12889096192 | bytes 42467328 | tf_op jit(solution)/shard_map/dot_general | solution.py:12
  807.3 31.7 %all-gather.15.cloned.1.call-done = f32[1,256,8192]{2,1,0:T(8,128)} async-done(((f32[1,64,8192]{2,1,0:T(8,128)}), f32[1,256,8192]{2,1,0:T(8,128)}) %all-gather.15.cloned.1.call-update) | async-done | bytes 8388624 | tf_op jit(solution)/shard_map/all_gather | solution.py:26
  839.0 18.4 %fusion.18 = f32[256,512]{0,1:T(8,128)} fusion(f32[512,8192]{1,0:T(8,128)} %convolution_subtract_fusion, f32[1,256,8192]{2,1,0:T(8,128)} %all-gather.15.cloned.1.call-done), kind=kOutput, calls=%fused_computation.19 | convolution fusion | flops 12884901888 | bytes 25690112 | tf_op jit(solution)/shard_map/dot_general | solution.py:8
  857.4 72.5 %all-reduce.11.cloned.1.call-done = f32[256,512]{0,1:T(8,128)} async-done(((f32[256,512]{0,1:T(8,128)}), f32[256,512]{0,1:T(8,128)}) %all-reduce.11.cloned.1.call-update) | async-done | bytes 524304 | tf_op jit(solution)/shard_map/psum | solution.py:28
  930.0 1.7 fusion.21
  931.6 26.0 %subtract_bitcast_fusion = f32[8192,512]{0,1:T(8,128)} fusion(f32[512,8192]{1,0:T(8,128)} %convolution_subtract_fusion, f32[512,256]{1,0:T(8,128)S(1)} %fusion.21, f32[1,256,8192]{2,1,0:T(8,128)} %all-gather.15.cloned.1.call-done), kind=kOutput, calls=%fused_computation.1 | convolution fusion | flops 12889096192 | bytes 42467328 | tf_op jit(solution)/shard_map/dot_general | solution.py:12
  957.6 17.4 %copy.5 = f32[8192,512]{1,0:T(8,128)} copy(f32[8192,512]{0,1:T(8,128)} %subtract_bitcast_fusion) | data formatting | bytes 33554432 | tf_op jit(solution)/shard_map/sub | solution.py:30
  (11 shorter events, 0.2 us)
Async XLA Ops:
  18.2 370.3 %all-to-all-start = ((f32[64,8,8192]{2,0,1:T(8,128)}), f32[64,8,8192]{2,0,1:T(8,128)}, u32[]{:S(2)}, u32[]{:S(2)}) async-start(f32[64,8,8192]{2,0,1:T(8,128)} %bitcast.65), calls=%async_computation | async-start | bytes 33554432 | tf_op jit(solution)/shard_map/all_to_all | solution.py:22
  25.5 66.8 %all-gather.9.cloned.1.call-start = ((), (), s32[]{:S(2)}) async-start(), calls=%async_computation.5 | async-start | bytes 10485760 | tf_op jit(solution)/shard_map/all_gather | solution.py:26
  32.4 447.1 %all-reduce.5.cloned.1.call-start = ((), (), s32[]{:S(2)}) async-start(), calls=%async_computation.1 | async-start | bytes 1048576 | tf_op jit(solution)/shard_map/psum | solution.py:28
  388.5 91.0 %copy-start = (f32[4,256,256]{2,1,0:T(8,128)S(1)}, f32[4,256,256]{2,1,0:T(8,128)}, u32[]{:S(2)}) copy-start(f32[4,256,256]{2,1,0:T(8,128)} %param.5) | copy-start | bytes 3145732
  408.0 130.8 %all-gather.11.cloned.1.call-start = ((), (), s32[]{:S(2)}) async-start(), calls=%async_computation.6 | async-start | bytes 10485760 | tf_op jit(solution)/shard_map/all_gather | solution.py:26
  408.7 221.0 %all-reduce.7.cloned.1.call-start = ((), (), s32[]{:S(2)}) async-start(), calls=%async_computation.2 | async-start | bytes 1048576 | tf_op jit(solution)/shard_map/psum | solution.py:28
  557.3 131.5 %all-gather.13.cloned.1.call-start = ((), (), s32[]{:S(2)}) async-start(), calls=%async_computation.7 | async-start | bytes 10485760 | tf_op jit(solution)/shard_map/all_gather | solution.py:26
  557.9 221.9 %all-reduce.9.cloned.1.call-start = ((), (), s32[]{:S(2)}) async-start(), calls=%async_computation.3 | async-start | bytes 1048576 | tf_op jit(solution)/shard_map/psum | solution.py:28
  707.2 131.8 %all-gather.15.cloned.1.call-start = ((), (), s32[]{:S(2)}) async-start(), calls=%async_computation.8 | async-start | bytes 10485760 | tf_op jit(solution)/shard_map/all_gather | solution.py:26
  707.9 222.0 %all-reduce.11.cloned.1.call-start = ((), (), s32[]{:S(2)}) async-start(), calls=%async_computation.4 | async-start | bytes 1048576 | tf_op jit(solution)/shard_map/psum | solution.py:28
Sparse Core Ops, SparseCore 0:
  32.6 59.6 all-gather.8
  408.1 71.3 all-reduce.4
  481.2 57.5 all-gather.10
  557.4 72.2 all-reduce.6
  631.1 57.5 all-gather.12
  707.3 72.3 all-reduce.8
  781.4 57.5 all-gather.14
  857.5 72.3 all-reduce.10
where the time goes:
time: 988 us; the launch traced here: 982 us
  waiting for transfers between devices  739 us (75%)
  matrix products  185 us (19%)
  local copies, waits for them, and re-layouts  36 us (4%)
  between operations  13.7 us (1%)
    all_to_all x1, waiting for transfers between devices, body(): lax.all_to_all(eigvecs, 'row', split_axis=1, concat_axis=0, tiled=True)  296 us
    psum x4, waiting for transfers between devices, body(): inner_sum = lax.psum(inner_part, 'row')  286 us
    all_gather x4, waiting for transfers between devices, body(): vectors = lax.all_gather(reflectors[block], 'col', axis=0, tiled=True)  154 us
    dot_general x4, matrix products, inner_rows(): lax.dot_general(left, right, (((0,), (0,)), ((), ())), precision=lax.Prec...  104 us
    dot_general x8, matrix products, matmul(): jnp.dot(left, right, precision=lax.Precision.HIGHEST, preferred_element_t...  81.7 us
  transfers between devices with their start and end apart: 9, of which 9 were waited for; matrix products, arithmetic and copies ran while one was open for 9% of the time, Pallas kernels for 0%

commit v1 on v0

v1 whole, which is shorter than its diff:
```python
import functools

import jax
import jax.numpy as jnp
from jax import lax
from jax.experimental import pallas as pl
from jax.experimental.pallas import tpu as pltpu
from jax.sharding import PartitionSpec as P

MESH = pl.DeviceIdType.MESH
PARTS = 4
TILE = 512


def split(value):
    high = value.astype(jnp.bfloat16)
    low = (value - high.astype(jnp.float32)).astype(jnp.bfloat16)
    return high, low


def product(left, right, dims):
    def one(a, b):
        return lax.dot_general(a, b, (dims, ((), ())), preferred_element_type=jnp.float32)

    return one(left[0], right[0]) + (one(left[0], right[1]) + one(left[1], right[0]))


def exact(left, right):
    return jnp.dot(left, right, precision=lax.Precision.HIGHEST, preferred_element_type=jnp.float32)


def allreduce(total, landed, full, send_sems, recv_sems, me, count):
    size = total.shape[0]
    offset = 0
    at = 0
    steps = []
    bit = 1
    index = 0
    while bit < count:
        size //= 2
        mine = lax.rem(me // bit, 2)
        partner = me + bit - 2 * bit * mine
        keep = pl.multiple_of(offset + mine * size, 8)
        give = pl.multiple_of(offset + (1 - mine) * size, 8)
        copy = pltpu.make_async_remote_copy(
            src_ref=total.at[pl.ds(give, size)],
            dst_ref=landed.at[pl.ds(at, size)],
            send_sem=send_sems.at[index],
            recv_sem=recv_sems.at[index],
            device_id={"row": partner},
            device_id_type=MESH,
        )
        copy.start()
        copy.wait()
        total[pl.ds(keep, size)] += landed[pl.ds(at, size)]
        steps.append((partner, keep, size))
        at += size
        offset = keep
        bit *= 2
        index += 1
    partner, keep, size = steps[-1]
    full[pl.ds(keep, size)] = total[pl.ds(keep, size)]
    for partner, keep, size in reversed(steps):
        piece = full.at[pl.ds(keep, size)]
        copy = pltpu.make_async_remote_copy(
            src_ref=piece,
            dst_ref=piece,
            send_sem=send_sems.at[index],
            recv_sem=recv_sems.at[index],
            device_id={"row": partner},
            device_id_type=MESH,
        )
        copy.start()
        copy.wait()
        index += 1


def kernel(
    shapes, eig, refl, tf, out, arrived, vec, gram, gram_in, gram_full, inner, inner_in, inner_full,
    scaled, scaled_hi, scaled_lo, x_send, x_recv, v_send, v_recv, r_send, r_recv, local,
):
    rows_n, cols_n = shapes
    row, col = lax.axis_index("row"), lax.axis_index("col")
    own, length = eig.shape[0], eig.shape[1] // rows_n
    blocks, _, share, _ = vec.shape
    nb = share * cols_n
    width = blocks * nb
    pairs = cols_n // 2
    core, place = lax.rem(col, 2), col // 2
    sibling = col + 1 - 2 * core
    step = own // PARTS
    nt = ((1,), (1,))

    barrier = pltpu.get_barrier_semaphore()
    for d in range(1, rows_n):
        pl.semaphore_signal(barrier, inc=1, device_id={"row": lax.rem(row + d, rows_n)}, device_id_type=MESH)
    for d in range(1, pairs):
        pl.semaphore_signal(barrier, inc=1, device_id={"col": lax.rem(place + d, pairs) * 2 + core}, device_id_type=MESH)
    pl.semaphore_signal(barrier, inc=1, device_id={"col": sibling}, device_id_type=MESH)
    pl.semaphore_wait(barrier, rows_n - 1 + pairs)

    def v_copy(src, slot, block, kind, target):
        copy = pltpu.make_async_remote_copy(
            src_ref=src,
            dst_ref=vec.at[block, slot],
            send_sem=v_send.at[block, kind],
            recv_sem=v_recv.at[block, kind],
            device_id={"col": target},
            device_id_type=MESH,
        )
        copy.start()
        return copy

    def x_start(part):
        copies = []
        for d in range(1, rows_n):
            target = lax.rem(row + d, rows_n)
            copy = pltpu.make_async_remote_copy(
                src_ref=eig.at[pl.ds(part * step, step), pl.ds(pl.multiple_of(target * length, 128), length)],
                dst_ref=arrived.at[row, pl.ds(part * step, step)],
                send_sem=x_send.at[part, d],
                recv_sem=x_recv.at[part, d],
                device_id={"row": target},
                device_id_type=MESH,
            )
            copy.start()
            copies.append(copy)
        return copies

    v_copies = []
    for b in range(blocks):
        direct = [v_copy(refl.at[b], col, b, d, lax.rem(place + d, pairs) * 2 + core) for d in range(1, pairs)]
        v_copies.append(direct)
    x_copies = [x_start(0), x_start(1)] + [None] * (PARTS - 2)
    near = [v_copy(refl.at[b], col, b, 0, sibling) for b in range(blocks)]
    v_local = pltpu.make_async_copy(refl, vec.at[:, col], local.at[0])
    v_local.start()
    x_local = pltpu.make_async_copy(
        eig.at[:, pl.ds(pl.multiple_of(row * length, 128), length)], arrived.at[row], local.at[1]
    )
    x_local.start()

    forwards = []
    for b in range(blocks):
        for d in range(1, pairs):
            v_copies[b][d - 1].wait_recv()
            slot = lax.rem(place + pairs - d, pairs) * 2 + core
            forwards.append(v_copy(vec.at[b, slot], slot, b, pairs + d - 1, sibling))
        if b == 1:
            x_copies[2] = x_start(2)
        if b == blocks - 1:
            x_copies[3] = x_start(3)
    v_local.wait()
    for copy in near + forwards:
        copy.wait()
    for direct in v_copies:
        for copy in direct:
            copy.wait_send()

    def vectors(start):
        tile = vec[:, :, :, pl.ds(pl.multiple_of(start, TILE), TILE)]
        return split(tile.reshape(width, TILE))

    gram[...] = jnp.zeros_like(gram)

    @pl.loop(0, length // TILE)
    def _(t):
        high, low = vectors(t * TILE)
        at = 0
        for i in range(blocks - 1):
            left = (high[i * nb : (i + 1) * nb], low[i * nb : (i + 1) * nb])
            for j in range(i + 1, blocks):
                right = (high[j * nb : (j + 1) * nb], low[j * nb : (j + 1) * nb])
                gram[pl.ds(at, nb)] += product(left, right, nt)
                at += nb

    allreduce(gram, gram_in, gram_full, r_send.at[PARTS], r_recv.at[PARTS], row, rows_n)
    x_local.wait()

    for part in range(PARTS):
        for copy in x_copies[part]:
            copy.wait()
        inner[...] = jnp.zeros_like(inner)


        def add_inner(x_ref):
            t = pl.program_id(0)
            piece = split(x_ref[...].reshape(rows_n * step, TILE))
            inner[...] += product(vectors(t * TILE), piece, nt)

        pltpu.emit_pipeline(
            add_inner,
            grid=(length // TILE,),
            in_specs=[pl.BlockSpec((rows_n, step, TILE), lambda t: (0, 0, t))],
            out_specs=[],
        )(arrived.at[:, pl.ds(part * step, step), :])
        allreduce(inner, inner_in, inner_full, r_send.at[part], r_recv.at[part], row, rows_n)
        found = [None] * blocks
        at = len(range(blocks)) * (blocks - 1) // 2 * nb
        for i in range(blocks - 1, -1, -1):
            term = inner_full[pl.ds(i * nb, nb)]
            at -= (blocks - 1 - i) * nb
            for j in range(i + 1, blocks):
                term = term - exact(gram_full[pl.ds(at + (j - i - 1) * nb, nb)], found[j])
            found[i] = exact(tf[i], term)
            scaled[:, pl.ds(part * step, step), pl.ds(i * nb, nb)] = found[i].T.reshape(rows_n, step, nb)

    high, low = split(scaled[...].reshape(rows_n * own, width))
    scaled_hi[...] = high
    scaled_lo[...] = low

    def finish(x_ref, out_ref):
        t = pl.program_id(0)
        change = product((scaled_hi[...], scaled_lo[...]), vectors(t * TILE), ((1,), (0,)))
        out_ref[...] = (x_ref[...].reshape(rows_n * own, TILE) - change).T

    pltpu.emit_pipeline(
        finish,
        grid=(length // TILE,),
        in_specs=[pl.BlockSpec((rows_n, own, TILE), lambda t: (0, 0, t))],
        out_specs=[pl.BlockSpec((TILE, rows_n * own), lambda t: (t, 0))],
    )(arrived, out)


def body(rows_n, cols_n, eigvecs, reflectors, tfactors):
    own, total = eigvecs.shape
    length = total // rows_n
    blocks, share, _ = reflectors.shape
    nb = share * cols_n
    width = blocks * nb
    wide = rows_n * own // PARTS
    grams = blocks * (blocks - 1) // 2 * nb
    steps = 2 * (rows_n.bit_length() - 1)
    f32, bf16 = jnp.float32, jnp.bfloat16
    hbm = pl.BlockSpec(memory_space=pl.ANY)
    result, _ = pl.pallas_call(
        functools.partial(kernel, (rows_n, cols_n)),
        out_shape=[
            jax.ShapeDtypeStruct((length, rows_n * own), f32),
            jax.ShapeDtypeStruct((rows_n, own, length), f32),
        ],
        in_specs=[hbm, hbm, pl.BlockSpec(memory_space=pltpu.VMEM)],
        out_specs=[hbm, hbm],
        scratch_shapes=[
            pltpu.VMEM((blocks, cols_n, share, length), f32),
            pltpu.VMEM((grams, nb), f32),
            pltpu.VMEM((grams, nb), f32),
            pltpu.VMEM((grams, nb), f32),
            pltpu.VMEM((width, wide), f32),
            pltpu.VMEM((width, wide), f32),
            pltpu.VMEM((width, wide), f32),
            pltpu.VMEM((rows_n, own, width), f32),
            pltpu.VMEM((rows_n * own, width), bf16),
            pltpu.VMEM((rows_n * own, width), bf16),
            pltpu.SemaphoreType.DMA((PARTS, rows_n)),
            pltpu.SemaphoreType.DMA((PARTS, rows_n)),
            pltpu.SemaphoreType.DMA((blocks, cols_n)),
            pltpu.SemaphoreType.DMA((blocks, cols_n)),
            pltpu.SemaphoreType.DMA((PARTS + 1, steps)),
            pltpu.SemaphoreType.DMA((PARTS + 1, steps)),
            pltpu.SemaphoreType.DMA((2,)),
        ],
        compiler_params=pltpu.CompilerParams(
            collective_id=0, has_side_effects=True, vmem_limit_bytes=60 * 1024 * 1024
        ),
    )(eigvecs, reflectors, tfactors)
    return result


def solution(mesh):
    in_specs = (P(("col", "row"), None), P(None, "col", "row"), P())
    out_specs = P("row", "col")
    part = functools.partial(body, mesh.shape["row"], mesh.shape["col"])
    return jax.shard_map(part, mesh=mesh, in_specs=in_specs, out_specs=out_specs, check_vma=False)
```

time: 988 us -> 656 us (0.66)
  waiting for transfers between devices: 739 us -> 0 us
  Pallas kernels: 0 us -> 643 us
  matrix products: 185 us -> 0 us
  local copies, waits for them, and re-layouts: 36 us -> 11.8 us
  between operations: 13.7 us -> 0.01 us
    pallas_call x0 -> x1, Pallas kernels: none -> 643 us  [body(): pl.pallas_call(functools.partial(kernel, (rows_n, cols_n)), out_shape=[ja...]
    all_to_all x1 -> x0, waiting for transfers between devices: 296 us -> none  [body(): lax.all_to_all(eigvecs, 'row', split_axis=1, concat_axis=0, tiled=True)]
    psum x4 -> x0, waiting for transfers between devices: 286 us -> none  [body(): inner_sum = lax.psum(inner_part, 'row')]
    dot_general x12 -> x0, matrix products: 185 us -> none  [the longest x4 104 us: inner_rows(): lax.dot_general(left, right, (((0,), (0,)), ((), ())), precision=lax.Prec...]
    all_gather x4 -> x0, waiting for transfers between devices: 154 us -> none  [body(): vectors = lax.all_gather(reflectors[block], 'col', axis=0, tiled=True)]
    sub x1 -> x0, local copies, waits for them, and re-layouts: 17.4 us -> none  [body(): current = current - inner_rows(vectors, scaled)]
    unnamed x2 -> x1, local copies, waits for them, and re-layouts: 0.01 us -> 11.8 us
    all_to_all x1 -> x0, local copies, waits for them, and re-layouts: 11.7 us -> none  [body(): lax.all_to_all(eigvecs, 'row', split_axis=1, concat_axis=0, tiled=True)]
  transfers between devices with their start and end apart: 9 -> 0, of which waited for: 9 -> 0; matrix products, arithmetic and copies ran while one was open for 9% -> 0% of each run, Pallas kernels for 0% -> 0%
where the time goes in v1:
time: 656 us; the launch traced here: 655 us
  Pallas kernels  643 us (98%)
  local copies, waits for them, and re-layouts  11.8 us (2%)
    pallas_call x1, Pallas kernels, body(): pl.pallas_call(functools.partial(kernel, (rows_n, cols_n)), out_shape=[ja...  643 us

profile of v1, /device:TPU:0, one launch (start us, length us, event | category | flops | bytes accessed | tf_op | source)
XLA Modules:
  0.0 655.0 jit_solution(18317998131870605532)
XLA Ops:
  0.0 643.3 %shard_map.37 = (f32[8192,512]{1,0:T(8,128)}, f32[8,64,8192]{2,1,0:T(8,128)}) custom-call(f32[64,65536]{1,0:T(8,128)} %eig.1, f32[4,64,8192]{2,1,0:T(8,128)} %refl.1, f32[4,256,256]{2,1,0:T(8,128)} %tf.1), custom_call_target="tpu_custom_call" | custom-call | tf_op jit(solution)/shard_map/pallas_call | solution.py:236
  643.3 11.8 %copy.5 = f32[8192,512]{1,0:T(8,128)} copy(f32[8192,512]{1,0:T(8,128)} %get-tuple-element.6) | data formatting | bytes 33554432

commit v2 on v1

--- a/solution.py
+++ b/solution.py
@@ -51,6 +51,7 @@
             device_id_type=MESH,
         )
         copy.start()
+        yield
         copy.wait()
         total[pl.ds(keep, size)] += landed[pl.ds(at, size)]
         steps.append((partner, keep, size))
@@ -71,12 +72,13 @@
             device_id_type=MESH,
         )
         copy.start()
+        yield
         copy.wait()
         index += 1
 
 
 def kernel(
-    shapes, eig, refl, tf, out, arrived, vec, gram, gram_in, gram_full, inner, inner_in, inner_full,
+    shapes, eig, refl, tf, out, arrived, vec, gram, gram_in, gram_full, held, inner, inner_in, inner_full,
     scaled, scaled_hi, scaled_lo, x_send, x_recv, v_send, v_recv, r_send, r_recv, local,
 ):
     rows_n, cols_n = shapes
@@ -113,7 +115,7 @@
 
     def x_start(part):
         copies = []
-        for d in range(1, rows_n):
+        for d in sorted(range(1, rows_n), key=lambda d: abs(2 * d - rows_n)):
             target = lax.rem(row + d, rows_n)
             copy = pltpu.make_async_remote_copy(
                 src_ref=eig.at[pl.ds(part * step, step), pl.ds(pl.multiple_of(target * length, 128), length)],
@@ -131,7 +133,7 @@
     for b in range(blocks):
         direct = [v_copy(refl.at[b], col, b, d, lax.rem(place + d, pairs) * 2 + core) for d in range(1, pairs)]
         v_copies.append(direct)
-    x_copies = [x_start(0), x_start(1)] + [None] * (PARTS - 2)
+    x_copies = [x_start(0), x_start(1), x_start(2), None]
     near = [v_copy(refl.at[b], col, b, 0, sibling) for b in range(blocks)]
     v_local = pltpu.make_async_copy(refl, vec.at[:, col], local.at[0])
     v_local.start()
@@ -140,70 +142,84 @@
     )
     x_local.start()
 
-    forwards = []
+    v_local.wait()
+    gram[...] = jnp.zeros_like(gram)
+
+    def vectors(start, first=0, last=blocks):
+        tile = vec[first:last, :, :, pl.ds(pl.multiple_of(start, TILE), TILE)]
+        return split(tile.reshape((last - first) * nb, TILE))
+
+    def pair(i, j):
+        return (i * (2 * blocks - 1 - i) // 2 + j - i - 1) * nb
+
     for b in range(blocks):
+        forwards = []
         for d in range(1, pairs):
             v_copies[b][d - 1].wait_recv()
             slot = lax.rem(place + pairs - d, pairs) * 2 + core
             forwards.append(v_copy(vec.at[b, slot], slot, b, pairs + d - 1, sibling))
         if b == 1:
-            x_copies[2] = x_start(2)
-        if b == blocks - 1:
             x_copies[3] = x_start(3)
-    v_local.wait()
-    for copy in near + forwards:
-        copy.wait()
+        near[b].wait()
+        for copy in forwards:
+            copy.wait()
+        if b > 0:
+
+            @pl.loop(0, length // TILE)
+            def _(t):
+                left = vectors(t * TILE, 0, b)
+                found = product(left, vectors(t * TILE, b, b + 1), nt)
+                for i in range(b):
+                    gram[pl.ds(pair(i, b), nb)] += found[i * nb : (i + 1) * nb]
+
     for direct in v_copies:
         for copy in direct:
             copy.wait_send()
 
-    def vectors(start):
-        tile = vec[:, :, :, pl.ds(pl.multiple_of(start, TILE), TILE)]
-        return split(tile.reshape(width, TILE))
-
-    gram[...] = jnp.zeros_like(gram)
-
-    @pl.loop(0, length // TILE)
-    def _(t):
-        high, low = vectors(t * TILE)
-        at = 0
-        for i in range(blocks - 1):
-            left = (high[i * nb : (i + 1) * nb], low[i * nb : (i + 1) * nb])
+    def solve(part):
+        found = [None] * blocks
+        for i in range(blocks - 1, -1, -1):
+            term = inner_full[pl.ds(i * nb, nb)]
             for j in range(i + 1, blocks):
-                right = (high[j * nb : (j + 1) * nb], low[j * nb : (j + 1) * nb])
-                gram[pl.ds(at, nb)] += product(left, right, nt)
-                at += nb
-
-    allreduce(gram, gram_in, gram_full, r_send.at[PARTS], r_recv.at[PARTS], row, rows_n)
+                term = term - exact(gram_full[pl.ds(pair(i, j), nb)], found[j])
+            found[i] = exact(tf[i], term)
+            scaled[:, pl.ds(part * step, step), pl.ds(i * nb, nb)] = found[i].T.reshape(rows_n, step, nb)
+
+    tiles = length // TILE
+    stops = 2 * (rows_n.bit_length() - 1)
     x_local.wait()
-
+    pending = allreduce(gram, gram_in, gram_full, r_send.at[PARTS], r_recv.at[PARTS], row, rows_n)
+    next(pending)
     for part in range(PARTS):
+        if part >= 2:
+            for _ in pending:
+                pass
+            solve(part - 1)
         for copy in x_copies[part]:
             copy.wait()
-        inner[...] = jnp.zeros_like(inner)
-
-
-        def add_inner(x_ref):
-            t = pl.program_id(0)
-            piece = split(x_ref[...].reshape(rows_n * step, TILE))
-            inner[...] += product(vectors(t * TILE), piece, nt)
-
-        pltpu.emit_pipeline(
-            add_inner,
-            grid=(length // TILE,),
-            in_specs=[pl.BlockSpec((rows_n, step, TILE), lambda t: (0, 0, t))],
-            out_specs=[],
-        )(arrived.at[:, pl.ds(part * step, step), :])
-        allreduce(inner, inner_in, inner_full, r_send.at[part], r_recv.at[part], row, rows_n)
-        found = [None] * blocks
-        at = len(range(blocks)) * (blocks - 1) // 2 * nb
-        for i in range(blocks - 1, -1, -1):
-            term = inner_full[pl.ds(i * nb, nb)]
-            at -= (blocks - 1 - i) * nb
-            for j in range(i + 1, blocks):
-                term = term - exact(gram_full[pl.ds(at + (j - i - 1) * nb, nb)], found[j])
-            found[i] = exact(tf[i], term)
-            scaled[:, pl.ds(part * step, step), pl.ds(i * nb, nb)] = found[i].T.reshape(rows_n, step, nb)
+        load = pltpu.make_async_copy(arrived.at[:, pl.ds(part * step, step), :], held, local.at[2])
+        load.start()
+        total = inner.at[part % 2]
+        total[...] = jnp.zeros_like(total)
+        load.wait()
+        for stop in range(stops):
+
+            @pl.loop(tiles * stop // stops, tiles * (stop + 1) // stops)
+            def _(t):
+                start = pl.multiple_of(t * TILE, TILE)
+                piece = split(held[:, :, pl.ds(start, TILE)].reshape(rows_n * step, TILE))
+                total[...] += product(vectors(start), piece, nt)
+
+            next(pending, None)
+        for _ in pending:
+            pass
+        if part == 1:
+            solve(0)
+        pending = allreduce(total, inner_in, inner_full, r_send.at[part], r_recv.at[part], row, rows_n)
+        next(pending)
+    for _ in pending:
+        pass
+    solve(PARTS - 1)
 
     high, low = split(scaled[...].reshape(rows_n * own, width))
     scaled_hi[...] = high
@@ -246,7 +262,8 @@
             pltpu.VMEM((grams, nb), f32),
             pltpu.VMEM((grams, nb), f32),
             pltpu.VMEM((grams, nb), f32),
-            pltpu.VMEM((width, wide), f32),
+            pltpu.VMEM((rows_n, own // PARTS, length), f32),
+            pltpu.VMEM((2, width, wide), f32),
             pltpu.VMEM((width, wide), f32),
             pltpu.VMEM((width, wide), f32),
             pltpu.VMEM((rows_n, own, width), f32),
@@ -258,7 +275,7 @@
             pltpu.SemaphoreType.DMA((blocks, cols_n)),
             pltpu.SemaphoreType.DMA((PARTS + 1, steps)),
             pltpu.SemaphoreType.DMA((PARTS + 1, steps)),
-            pltpu.SemaphoreType.DMA((2,)),
+            pltpu.SemaphoreType.DMA((3,)),
         ],
         compiler_params=pltpu.CompilerParams(
             collective_id=0, has_side_effects=True, vmem_limit_bytes=60 * 1024 * 1024

time: 656 us -> 632 us (0.963); the launches traced: 655 us -> 623 us
  Pallas kernels: 643 us -> 611 us
    pallas_call x1, Pallas kernels: 643 us -> 611 us  [body(): pl.pallas_call(functools.partial(kernel, (rows_n, cols_n)), out_shape=[ja...]
where the time goes in v2:
time: 632 us; the launch traced here: 623 us
  Pallas kernels  611 us (97%)
  local copies, waits for them, and re-layouts  11.8 us (2%)
    pallas_call x1, Pallas kernels, body(): pl.pallas_call(functools.partial(kernel, (rows_n, cols_n)), out_shape=[ja...  611 us

profile of v2, /device:TPU:0, one launch (start us, length us, event | category | flops | bytes accessed | tf_op | source)
XLA Modules:
  0.0 623.2 jit_solution(534098626385916476)
XLA Ops:
  0.0 611.0 %shard_map.37 = (f32[8192,512]{1,0:T(8,128)}, f32[8,64,8192]{2,1,0:T(8,128)}) custom-call(f32[64,65536]{1,0:T(8,128)} %eig.1, f32[4,64,8192]{2,1,0:T(8,128)} %refl.1, f32[4,256,256]{2,1,0:T(8,128)} %tf.1), custom_call_target="tpu_custom_call" | custom-call | tf_op jit(solution)/shard_map/pallas_call | solution.py:252
  611.1 11.8 %copy.5 = f32[8192,512]{1,0:T(8,128)} copy(f32[8192,512]{1,0:T(8,128)} %get-tuple-element.6) | data formatting | bytes 33554432
